TPU v7x, 256 devices: a whole 4x4x8 slice. The times are simulated.
256 devices in a mesh: ckpt: 8 (over z_lo, y), tensor: 8 (over z_hi, core), ex: 4 (over x).
Axes of the slice: x: 4, y: 4, z: 8 (z_hi: 4, z_lo: 2; z = z_hi * 2 + z_lo), core: 2. Of those that a mesh axis runs over, the one named last changes fastest.
Arguments:
- x_train: bfloat16 [8, 512, 5120], P('ckpt', ('tensor', 'ex')), may hold values from -6 to 6
- dy_train: bfloat16 [8, 512, 5120], P('ckpt', ('tensor', 'ex')), may hold values from -6 to 6
- x_test: bfloat16 [8, 512, 5120], P('ckpt', ('tensor', 'ex')), may hold values from -6 to 6
- dy_test: bfloat16 [8, 512, 5120], P('ckpt', ('tensor', 'ex')), may hold values from -6 to 6
- gate_train: bfloat16 [8, 512, 13824], P('ckpt', None, ('tensor', 'ex')), may hold values from -8 to 8
- gate_test: bfloat16 [8, 512, 13824], P('ckpt', None, ('tensor', 'ex')), may hold values from -8 to 8
- w_up: bfloat16 [8, 5120, 13824], P('ckpt', None, ('tensor', 'ex')), may hold values from -0.078125 to 0.078125
- w_down: bfloat16 [8, 13824, 5120], P('ckpt', ('tensor', 'ex')), may hold values from -0.078125 to 0.078125
- proj_hidden: int32 [13824, 64], P(('tensor', 'ex')), may hold values from 0 to 1
- proj_model: int32 [5120, 64], replicated, may hold values from 0 to 1
- rates: float32 [8], P('ckpt'), may hold values from 0.25 to 4
Outputs:
- scores: float32 [4, 4], P('ex')
All inputs are finite; a program needn't handle non-finite values.
Results may differ from a plain program's by a relative error of at most 0.0038.
Values may be sent and summed in bfloat16 or wider, within the bound.
No kernel may reach another device: no remote copies, remote signals or barrier semaphores. Data moves between devices by JAX's collectives and lax.ppermute only.
A program may use at most 128 MiB of HBM per device.

v0:
```python
import jax
import jax.numpy as jnp
from jax import lax
from jax.sharding import PartitionSpec as P

D = 5120
FF = 13824
KF = 64
KD = 64
SEQ = 128


def block_factors(x, dy, gate, w_up, w_down, sign_h, sign_m):
    up = jnp.dot(x, w_up, preferred_element_type=jnp.float32)
    act = jax.nn.silu(gate.astype(jnp.float32))
    hidden = (act * up).astype(jnp.bfloat16)
    grad_hidden = lax.dot_general(
        dy, w_down, (((1,), (1,)), ((), ())), preferred_element_type=jnp.float32
    )
    grad_up = (grad_hidden * act).astype(jnp.bfloat16)
    hidden_side = jnp.concatenate(
        [
            jnp.dot(hidden, sign_h, preferred_element_type=jnp.float32),
            jnp.dot(grad_up, sign_h, preferred_element_type=jnp.float32),
        ],
        axis=1,
    ) * FF ** (-0.5)
    model_side = jnp.concatenate(
        [
            jnp.dot(dy, sign_m, preferred_element_type=jnp.float32),
            jnp.dot(x, sign_m, preferred_element_type=jnp.float32),
        ],
        axis=1,
    ) * D ** (-0.5)
    return (hidden_side, model_side)


def sketch_rows(hidden_side, model_side):
    left = hidden_side.reshape(-1, SEQ, 2 * KF)
    right = model_side.reshape(-1, SEQ, 2 * KD)
    down = (
        jnp.einsum(
            "nsk,nsl->nkl", left[:, :, :KF], right[:, :, :KD], precision=lax.Precision.HIGHEST
        )
        / SEQ
    )
    upper = (
        jnp.einsum(
            "nsk,nsl->nkl", right[:, :, KD:], left[:, :, KF:], precision=lax.Precision.HIGHEST
        )
        / SEQ
    )
    count = left.shape[0]
    return jnp.concatenate([down.reshape(count, -1), upper.reshape(count, -1)], axis=1)


def body(
    x_train,
    dy_train,
    x_test,
    dy_test,
    gate_train,
    gate_test,
    w_up,
    w_down,
    proj_hidden,
    proj_model,
    rates,
):
    pieces = (x_train[0], dy_train[0], x_test[0], dy_test[0])
    gathered = (
        lax.all_gather(pieces[0], ("tensor", "ex"), axis=0, tiled=True),
        lax.all_gather(pieces[1], ("tensor", "ex"), axis=0, tiled=True),
        lax.all_gather(pieces[2], ("tensor", "ex"), axis=0, tiled=True),
        lax.all_gather(pieces[3], ("tensor", "ex"), axis=0, tiled=True),
    )
    train_x, train_dy, test_x, test_dy = gathered
    sign_h = (2 * proj_hidden - 1).astype(jnp.bfloat16)
    sign_m = (2 * proj_model - 1).astype(jnp.bfloat16)
    train_h, train_m = block_factors(
        train_x, train_dy, gate_train[0], w_up[0], w_down[0], sign_h, sign_m
    )
    test_h, test_m = block_factors(
        test_x, test_dy, gate_test[0], w_up[0], w_down[0], sign_h, sign_m
    )
    train_count = train_x.shape[0] // SEQ
    per_device = train_count // lax.axis_size("ex")
    start = lax.axis_index("ex") * per_device
    train_h, test_h = lax.psum((train_h, test_h), ("tensor", "ex"))
    train_sketch = sketch_rows(train_h, train_m)
    test_sketch = sketch_rows(test_h, test_m)
    mine = lax.dynamic_slice_in_dim(train_sketch, start, per_device, 0)
    block = rates[0] * jnp.dot(
        mine, test_sketch.T, precision=lax.Precision.HIGHEST, preferred_element_type=jnp.float32
    )
    return lax.psum(block, "ckpt")


def solution(mesh):
    in_specs = (
        P("ckpt", ("tensor", "ex"), None),
        P("ckpt", ("tensor", "ex"), None),
        P("ckpt", ("tensor", "ex"), None),
        P("ckpt", ("tensor", "ex"), None),
        P("ckpt", None, ("tensor", "ex")),
        P("ckpt", None, ("tensor", "ex")),
        P("ckpt", None, ("tensor", "ex")),
        P("ckpt", ("tensor", "ex"), None),
        P(("tensor", "ex"), None),
        P(),
        P("ckpt"),
    )
    out_specs = P("ex", None)
    return jax.shard_map(body, mesh=mesh, in_specs=in_specs, out_specs=out_specs, check_vma=False)
```

profile of v0, /device:TPU:2, one launch (start us, length us, event | category | flops | bytes accessed | tf_op | source)
XLA Modules:
  0.0 596.8 jit_solution(1330427506890708722)
XLA Ops:
  6.5 0.0 all-gather.9.cloned.1.call-start
  6.5 0.7 all-gather.9.cloned.1.call-update
  7.3 0.0 all-gather.11.cloned.1.call-start
  7.3 0.7 all-gather.11.cloned.1.call-update
  8.0 0.0 all-gather.13.cloned.1.call-start
  8.1 0.7 all-gather.13.cloned.1.call-update
  8.7 0.0 all-gather.15.cloned.1.call-start
  8.8 0.5 all-gather.15.cloned.1.call-update
  9.3 0.0 all-reduce.3.cloned.1.call-start
  10.0 0.9 add_convert_fusion.1
  10.9 1.5 add_convert_fusion
  12.4 65.0 %all-gather.9.cloned.1.call-done = bf16[1,512,5120]{2,1,0:T(8,128)(2,1)} async-done(((bf16[1,16,5120]{2,1,0:T(8,128)(2,1)}), bf16[1,512,5120]{2,1,0:T(8,128)(2,1)}) %all-gather.9.cloned.1.call-update) | async-done | bytes 5242896 | tf_op jit(solution)/shard_map/all_gather | solution.py:72
  77.4 4.2 fusion.80
  81.6 0.0 copy-start
  81.6 60.7 %all-gather.11.cloned.1.call-done = bf16[1,512,5120]{2,1,0:T(8,128)(2,1)} async-done(((bf16[1,16,5120]{2,1,0:T(8,128)(2,1)}), bf16[1,512,5120]{2,1,0:T(8,128)(2,1)}) %all-gather.11.cloned.1.call-update) | async-done | bytes 5242896 | tf_op jit(solution)/shard_map/all_gather | solution.py:73
  142.3 4.2 fusion.83
  146.5 60.7 %all-gather.13.cloned.1.call-done = bf16[1,512,5120]{2,1,0:T(8,128)(2,1)} async-done(((bf16[1,16,5120]{2,1,0:T(8,128)(2,1)}), bf16[1,512,5120]{2,1,0:T(8,128)(2,1)}) %all-gather.13.cloned.1.call-update) | async-done | bytes 5242896 | tf_op jit(solution)/shard_map/all_gather | solution.py:74
  207.3 4.2 fusion.86
  211.5 0.0 copy-done
  211.5 6.5 %fusion.62 = f32[512,64]{0,1:T(8,128)S(1)} fusion(bf16[432,64]{0,1:T(8,128)(2,1)S(1)} %add_convert_fusion.1, bf16[1,5120,432]{1,2,0:T(8,128)(2,1)} %param.17, bf16[1,512,5120]{2,1,0:T(8,128)(2,1)} %all-gather.9.cloned.1.call-done, bf16[1,512,432]{1,2,0:T(8,128)(2,1)S(1)} %copy-done), kind=kOutput, calls=%fused_computation.29 | convolution fusion | flops 2294784000 | bytes 10295296 | tf_op jit(solution)/shard_map/dot_general | solution.py:23
  218.0 0.0 copy-start.1
  218.0 6.7 %fusion.67 = f32[512,64]{0,1:T(8,128)S(1)} fusion(bf16[432,64]{0,1:T(8,128)(2,1)S(1)} %add_convert_fusion.1, bf16[1,432,5120]{2,1,0:T(8,128)(2,1)} %param.18, bf16[1,512,5120]{2,1,0:T(8,128)(2,1)} %all-gather.11.cloned.1.call-done, bf16[1,512,432]{1,2,0:T(8,128)(2,1)S(1)} %copy-done), kind=kOutput, calls=%fused_computation.30 | convolution fusion | flops 2294784000 | bytes 10295296 | tf_op jit(solution)/shard_map/dot_general | solution.py:24
  224.8 0.0 copy-done.1
  224.8 6.6 %fusion.72 = f32[512,64]{0,1:T(8,128)S(1)} fusion(bf16[432,64]{0,1:T(8,128)(2,1)S(1)} %add_convert_fusion.1, bf16[1,5120,432]{1,2,0:T(8,128)(2,1)} %param.17, bf16[1,512,5120]{2,1,0:T(8,128)(2,1)} %all-gather.13.cloned.1.call-done, bf16[1,512,432]{1,2,0:T(8,128)(2,1)S(1)} %copy-done.1), kind=kOutput, calls=%fused_computation.31 | convolution fusion | flops 2294784000 | bytes 10295296 | tf_op jit(solution)/shard_map/dot_general | solution.py:23
  231.3 40.7 %all-gather.15.cloned.1.call-done = bf16[1,512,5120]{2,1,0:T(8,128)(2,1)} async-done(((bf16[1,16,5120]{2,1,0:T(8,128)(2,1)}), bf16[1,512,5120]{2,1,0:T(8,128)(2,1)}) %all-gather.15.cloned.1.call-update) | async-done | bytes 5242896 | tf_op jit(solution)/shard_map/all_gather | solution.py:75
  272.1 6.7 %fusion.77 = f32[512,64]{0,1:T(8,128)S(1)} fusion(bf16[432,64]{0,1:T(8,128)(2,1)S(1)} %add_convert_fusion.1, bf16[1,432,5120]{2,1,0:T(8,128)(2,1)} %param.18, bf16[1,512,5120]{2,1,0:T(8,128)(2,1)} %all-gather.15.cloned.1.call-done, bf16[1,512,432]{1,2,0:T(8,128)(2,1)S(1)} %copy-done.1), kind=kOutput, calls=%fused_computation.32 | convolution fusion | flops 2294784000 | bytes 10295296 | tf_op jit(solution)/shard_map/dot_general | solution.py:24
  278.8 0.9 copy_bitcast_fusion
  279.6 0.0 all-reduce.3.cloned.1.call-update
  279.7 4.2 fusion.89
  283.9 280.9 %all-reduce.3.cloned.1.call-done = (f32[4,128,128]{1,2,0:T(8,128)}, f32[4,128,128]{1,2,0:T(8,128)}) async-done(((f32[4,128,128]{1,2,0:T(8,128)}, f32[4,128,128]{1,2,0:T(8,128)}), (f32[4,128,128]{1,2,0:T(8,128)}, f32[4,128,128]{1,2,0:T(8,128)})) %all-reduce.3.cloned.1.call-update) | async-done | bytes 524304 | tf_op jit(solution)/shard_map/psum | solution.py:89
  564.8 1.2 convolution_multiply_fusion.3
  566.1 1.2 convolution_multiply_fusion.2
  567.3 1.2 convolution_multiply_fusion.1
  568.6 1.2 convolution_multiply_fusion
  569.8 0.1 reshape.34
  570.0 0.1 reshape.35
  570.1 0.1 reshape.38
  570.2 0.1 reshape.39
  570.3 0.7 fusion.93
  570.9 19.3 %psum.23 = f32[1,4]{1,0:T(1,128)} all-reduce(f32[1,4]{1,0:T(1,128)S(1)} %fusion.93), channel_id=1, replica_groups=mesh['ckpt'=8,'tensor'=8,'ex'=4] {'ckpt'}, use_global_device_ids=true, to_apply=%region_2.3 | all-reduce | flops 4 | bytes 32 | tf_op jit(solution)/shard_map/psum | solution.py:96
  (6 shorter events, 0.1 us)
Async XLA Ops:
  6.5 70.8 %all-gather.9.cloned.1.call-start = ((), (), s32[]{:S(2)}) async-start(), calls=%async_computation | async-start | bytes 5406720 | tf_op jit(solution)/shard_map/all_gather | solution.py:72
  7.3 135.1 %all-gather.11.cloned.1.call-start = ((), (), s32[]{:S(2)}) async-start(), calls=%async_computation.1 | async-start | bytes 5406720 | tf_op jit(solution)/shard_map/all_gather | solution.py:73
  8.0 199.3 %all-gather.13.cloned.1.call-start = ((), (), s32[]{:S(2)}) async-start(), calls=%async_computation.2 | async-start | bytes 5406720 | tf_op jit(solution)/shard_map/all_gather | solution.py:74
  8.7 263.3 %all-gather.15.cloned.1.call-start = ((), (), s32[]{:S(2)}) async-start(), calls=%async_computation.3 | async-start | bytes 5406720 | tf_op jit(solution)/shard_map/all_gather | solution.py:75
  9.3 555.5 %all-reduce.3.cloned.1.call-start = ((), (), s32[]{:S(2)}) async-start(), calls=%async_computation.4 | async-start | bytes 1048576 | tf_op jit(solution)/shard_map/psum | solution.py:89
  81.6 129.9 %copy-start = (bf16[1,512,432]{1,2,0:T(8,128)(2,1)S(1)}, bf16[1,512,432]{1,2,0:T(8,128)(2,1)}, u32[]{:S(2)}) copy-start(bf16[1,512,432]{1,2,0:T(8,128)(2,1)} %param.15) | copy-start | bytes 1327108
  218.0 6.7 %copy-start.1 = (bf16[1,512,432]{1,2,0:T(8,128)(2,1)S(1)}, bf16[1,512,432]{1,2,0:T(8,128)(2,1)}, u32[]{:S(2)}) copy-start(bf16[1,512,432]{1,2,0:T(8,128)(2,1)} %param.16) | copy-start | bytes 1327108
Sparse Core Ops, SparseCore 0:
  9.9 67.4 all-gather.8
  79.9 62.3 all-gather.10
  144.9 62.3 all-gather.12
  209.7 62.3 all-gather.14
  279.8 284.9 all-reduce.2
where the time goes:
time: 597 us
  waiting for transfers between devices  511 us (86%)
  matrix products  49 us (8%)
  blocking collectives  19.3 us (3%)
  between operations  13.9 us (2%)
    psum x1, waiting for transfers between devices, body(): train_h, test_h = lax.psum((train_h, test_h), ('tensor', 'ex'))  281 us
    all_gather x1, waiting for transfers between devices, body(): lax.all_gather(pieces[0], ('tensor', 'ex'), axis=0, tiled=True)  65 us
    all_gather x1, waiting for transfers between devices, body(): lax.all_gather(pieces[2], ('tensor', 'ex'), axis=0, tiled=True)  60.7 us
    all_gather x1, waiting for transfers between devices, body(): lax.all_gather(pieces[1], ('tensor', 'ex'), axis=0, tiled=True)  60.7 us
    all_gather x1, waiting for transfers between devices, body(): lax.all_gather(pieces[3], ('tensor', 'ex'), axis=0, tiled=True)  40.7 us
    psum x1, blocking collectives, body(): return lax.psum(block, 'ckpt')  19.3 us
    dot_general x2, matrix products, block_factors(): jnp.dot(grad_up, sign_h, preferred_element_type=jnp.float32)  13.4 us
    dot_general x2, matrix products, block_factors(): jnp.dot(hidden, sign_h, preferred_element_type=jnp.float32)  13.1 us
  transfers between devices with their start and end apart: 5, of which 5 were waited for; matrix products, arithmetic and copies ran while one was open for 7% of the time, Pallas kernels for 0%

commit v1 on v0

--- a/solution.py
+++ b/solution.py
@@ -8,6 +8,11 @@
 KF = 64
 KD = 64
 SEQ = 128
+
+
+def by_each_axis(value, axis_one, axis_two):
+    half = lax.psum(value, axis_one)
+    return lax.psum(half, axis_two)
 
 
 def block_factors(x, dy, gate, w_up, w_down, sign_h, sign_m):
@@ -86,7 +91,7 @@
     train_count = train_x.shape[0] // SEQ
     per_device = train_count // lax.axis_size("ex")
     start = lax.axis_index("ex") * per_device
-    train_h, test_h = lax.psum((train_h, test_h), ("tensor", "ex"))
+    train_h, test_h = by_each_axis((train_h, test_h), "ex", "tensor")
     train_sketch = sketch_rows(train_h, train_m)
     test_sketch = sketch_rows(test_h, test_m)
     mine = lax.dynamic_slice_in_dim(train_sketch, start, per_device, 0)

time: 597 us -> 435 us (0.73)
  waiting for transfers between devices: 511 us -> 346 us
    psum x1 -> x2, waiting for transfers between devices: 281 us -> 104 us  [the longest x1 72.1 us: by_each_axis(): return lax.psum(half, axis_two)]
    all_gather x1, waiting for transfers between devices: 40.7 us -> 58.3 us  [body(): lax.all_gather(pieces[3], ('tensor', 'ex'), axis=0, tiled=True)]
  transfers between devices with their start and end apart: 5 -> 6, of which waited for: 5 -> 6; matrix products, arithmetic and copies ran while one was open for 7% -> 9% of each run, Pallas kernels for 0% -> 0%
where the time goes in v1:
time: 435 us
  waiting for transfers between devices  346 us (80%)
  matrix products  48.5 us (11%)
  blocking collectives  19.2 us (4%)
  between operations  14.2 us (3%)
    psum x1, waiting for transfers between devices, by_each_axis(): return lax.psum(half, axis_two)  72.1 us
    all_gather x1, waiting for transfers between devices, body(): lax.all_gather(pieces[0], ('tensor', 'ex'), axis=0, tiled=True)  64.9 us
    all_gather x1, waiting for transfers between devices, body(): lax.all_gather(pieces[1], ('tensor', 'ex'), axis=0, tiled=True)  58.4 us
    all_gather x1, waiting for transfers between devices, body(): lax.all_gather(pieces[3], ('tensor', 'ex'), axis=0, tiled=True)  58.3 us
    all_gather x1, waiting for transfers between devices, body(): lax.all_gather(pieces[2], ('tensor', 'ex'), axis=0, tiled=True)  57.7 us
    psum x1, waiting for transfers between devices, by_each_axis(): half = lax.psum(value, axis_one)  32.3 us
    psum x1, blocking collectives, body(): return lax.psum(block, 'ckpt')  19.2 us
    dot_general x2, matrix products, block_factors(): jnp.dot(hidden, sign_h, preferred_element_type=jnp.float32)  13 us
  transfers between devices with their start and end apart: 6, of which 6 were waited for; matrix products, arithmetic and copies ran while one was open for 9% of the time, Pallas kernels for 0%

profile of v1, /device:TPU:2, one launch (start us, length us, event | category | flops | bytes accessed | tf_op | source)
XLA Modules:
  0.0 435.0 jit_solution(922996600056908757)
XLA Ops:
  6.5 0.0 all-gather.9.cloned.1.call-start
  6.5 0.7 all-gather.9.cloned.1.call-update
  7.3 0.0 all-gather.11.cloned.1.call-start
  7.3 0.7 all-gather.11.cloned.1.call-update
  8.0 0.0 all-gather.13.cloned.1.call-start
  8.1 0.7 all-gather.13.cloned.1.call-update
  8.7 0.0 all-gather.15.cloned.1.call-start
  8.8 0.5 all-gather.15.cloned.1.call-update
  9.3 0.0 all-reduce.7.cloned.1.call-start
  10.0 0.9 add_convert_fusion.1
  10.9 1.5 add_convert_fusion
  12.4 0.0 copy-start
  12.4 64.9 %all-gather.9.cloned.1.call-done = bf16[1,512,5120]{2,1,0:T(8,128)(2,1)} async-done(((bf16[1,16,5120]{2,1,0:T(8,128)(2,1)}), bf16[1,512,5120]{2,1,0:T(8,128)(2,1)}) %all-gather.9.cloned.1.call-update) | async-done | bytes 5242896 | tf_op jit(solution)/shard_map/all_gather | solution.py:77
  77.4 6.5 %fusion.62 = f32[512,64]{0,1:T(8,128)S(1)} fusion(bf16[432,64]{0,1:T(8,128)(2,1)S(1)} %add_convert_fusion.1, bf16[1,5120,432]{1,2,0:T(8,128)(2,1)} %param.17, bf16[1,512,5120]{2,1,0:T(8,128)(2,1)} %all-gather.9.cloned.1.call-done, bf16[1,512,432]{1,2,0:T(8,128)(2,1)} %param.15), kind=kOutput, calls=%fused_computation.29 | convolution fusion | flops 2294784000 | bytes 10295296 | tf_op jit(solution)/shard_map/dot_general | solution.py:28
  83.9 0.0 copy-start.1
  83.9 58.4 %all-gather.11.cloned.1.call-done = bf16[1,512,5120]{2,1,0:T(8,128)(2,1)} async-done(((bf16[1,16,5120]{2,1,0:T(8,128)(2,1)}), bf16[1,512,5120]{2,1,0:T(8,128)(2,1)}) %all-gather.11.cloned.1.call-update) | async-done | bytes 5242896 | tf_op jit(solution)/shard_map/all_gather | solution.py:78
  142.3 0.0 copy-done
  142.3 6.5 %fusion.67 = f32[512,64]{0,1:T(8,128)S(1)} fusion(bf16[432,64]{0,1:T(8,128)(2,1)S(1)} %add_convert_fusion.1, bf16[1,432,5120]{2,1,0:T(8,128)(2,1)} %param.18, bf16[1,512,5120]{2,1,0:T(8,128)(2,1)} %all-gather.11.cloned.1.call-done, bf16[1,512,432]{1,2,0:T(8,128)(2,1)S(1)} %copy-done), kind=kOutput, calls=%fused_computation.30 | convolution fusion | flops 2294784000 | bytes 10295296 | tf_op jit(solution)/shard_map/dot_general | solution.py:29
  148.8 0.8 maximum_multiply_fusion
  149.6 57.7 %all-gather.13.cloned.1.call-done = bf16[1,512,5120]{2,1,0:T(8,128)(2,1)} async-done(((bf16[1,16,5120]{2,1,0:T(8,128)(2,1)}), bf16[1,512,5120]{2,1,0:T(8,128)(2,1)}) %all-gather.13.cloned.1.call-update) | async-done | bytes 5242896 | tf_op jit(solution)/shard_map/all_gather | solution.py:79
  207.3 0.0 copy-done.1
  207.3 6.5 %fusion.72 = f32[512,64]{0,1:T(8,128)S(1)} fusion(bf16[432,64]{0,1:T(8,128)(2,1)S(1)} %add_convert_fusion.1, bf16[1,5120,432]{1,2,0:T(8,128)(2,1)} %param.17, bf16[1,512,5120]{2,1,0:T(8,128)(2,1)} %all-gather.13.cloned.1.call-done, bf16[1,512,432]{1,2,0:T(8,128)(2,1)S(1)} %copy-done.1), kind=kOutput, calls=%fused_computation.31 | convolution fusion | flops 2294784000 | bytes 10295296 | tf_op jit(solution)/shard_map/dot_general | solution.py:28
  213.8 58.3 %all-gather.15.cloned.1.call-done = bf16[1,512,5120]{2,1,0:T(8,128)(2,1)} async-done(((bf16[1,16,5120]{2,1,0:T(8,128)(2,1)}), bf16[1,512,5120]{2,1,0:T(8,128)(2,1)}) %all-gather.15.cloned.1.call-update) | async-done | bytes 5242896 | tf_op jit(solution)/shard_map/all_gather | solution.py:80
  272.1 6.5 %fusion.77 = f32[512,64]{0,1:T(8,128)S(1)} fusion(bf16[432,64]{0,1:T(8,128)(2,1)S(1)} %add_convert_fusion.1, bf16[1,432,5120]{2,1,0:T(8,128)(2,1)} %param.18, bf16[1,512,5120]{2,1,0:T(8,128)(2,1)} %all-gather.15.cloned.1.call-done, bf16[1,512,432]{1,2,0:T(8,128)(2,1)S(1)} %copy-done.1), kind=kOutput, calls=%fused_computation.32 | convolution fusion | flops 2294784000 | bytes 10295296 | tf_op jit(solution)/shard_map/dot_general | solution.py:29
  278.6 0.7 maximum_multiply_fusion.2
  279.3 0.0 all-reduce.7.cloned.1.call-update
  279.3 0.2 all-reduce.5.cloned.1.call-start
  279.6 4.2 fusion.80
  283.8 4.2 fusion.83
  288.0 4.2 fusion.86
  292.2 32.3 %all-reduce.7.cloned.1.call-done = (f32[512,128]{0,1:T(8,128)}, f32[512,128]{0,1:T(8,128)}) async-done(((f32[512,128]{0,1:T(8,128)}, f32[512,128]{0,1:T(8,128)}), (f32[512,128]{0,1:T(8,128)}, f32[512,128]{0,1:T(8,128)})) %all-reduce.7.cloned.1.call-update) | async-done | bytes 524304 | tf_op jit(solution)/shard_map/psum | solution.py:14
  324.6 1.9 copy_bitcast_fusion
  326.5 0.0 all-reduce.5.cloned.1.call-update
  326.5 4.2 fusion.89
  330.8 72.1 %all-reduce.5.cloned.1.call-done = (f32[4,128,128]{1,2,0:T(8,128)}, f32[4,128,128]{1,2,0:T(8,128)}) async-done(((f32[4,128,128]{1,2,0:T(8,128)}, f32[4,128,128]{1,2,0:T(8,128)}), (f32[4,128,128]{1,2,0:T(8,128)}, f32[4,128,128]{1,2,0:T(8,128)})) %all-reduce.5.cloned.1.call-update) | async-done | bytes 524304 | tf_op jit(solution)/shard_map/psum | solution.py:15
  402.9 1.2 convolution_multiply_fusion.3
  404.1 1.2 convolution_multiply_fusion.2
  405.4 1.2 convolution_multiply_fusion.1
  406.6 1.2 convolution_multiply_fusion
  407.9 0.1 reshape.34
  408.0 0.1 reshape.35
  408.1 0.1 reshape.38
  408.2 0.1 reshape.39
  408.3 0.7 fusion.93
  409.0 19.2 %psum.39 = f32[1,4]{1,0:T(1,128)} all-reduce(f32[1,4]{1,0:T(1,128)S(1)} %fusion.93), channel_id=1, replica_groups=mesh['ckpt'=8,'tensor'=8,'ex'=4] {'ckpt'}, use_global_device_ids=true, to_apply=%region_4.5 | all-reduce | flops 4 | bytes 32 | tf_op jit(solution)/shard_map/psum | solution.py:101
  (6 shorter events, 0.1 us)
Async XLA Ops:
  6.5 70.8 %all-gather.9.cloned.1.call-start = ((), (), s32[]{:S(2)}) async-start(), calls=%async_computation | async-start | bytes 5406720 | tf_op jit(solution)/shard_map/all_gather | solution.py:77
  7.3 135.1 %all-gather.11.cloned.1.call-start = ((), (), s32[]{:S(2)}) async-start(), calls=%async_computation.1 | async-start | bytes 5406720 | tf_op jit(solution)/shard_map/all_gather | solution.py:78
  8.0 199.3 %all-gather.13.cloned.1.call-start = ((), (), s32[]{:S(2)}) async-start(), calls=%async_computation.2 | async-start | bytes 5406720 | tf_op jit(solution)/shard_map/all_gather | solution.py:79
  8.7 263.3 %all-gather.15.cloned.1.call-start = ((), (), s32[]{:S(2)}) async-start(), calls=%async_computation.3 | async-start | bytes 5406720 | tf_op jit(solution)/shard_map/all_gather | solution.py:80
  9.3 315.3 %all-reduce.7.cloned.1.call-start = ((), (), s32[]{:S(2)}) async-start(), calls=%async_computation.5 | async-start | bytes 1048576 | tf_op jit(solution)/shard_map/psum | solution.py:14
  12.4 129.9 %copy-start = (bf16[1,512,432]{1,2,0:T(8,128)(2,1)S(1)}, bf16[1,512,432]{1,2,0:T(8,128)(2,1)}, u32[]{:S(2)}) copy-start(bf16[1,512,432]{1,2,0:T(8,128)(2,1)} %param.15) | copy-start | bytes 1327108
  83.9 123.4 %copy-start.1 = (bf16[1,512,432]{1,2,0:T(8,128)(2,1)S(1)}, bf16[1,512,432]{1,2,0:T(8,128)(2,1)}, u32[]{:S(2)}) copy-start(bf16[1,512,432]{1,2,0:T(8,128)(2,1)} %param.16) | copy-start | bytes 1327108
  279.3 123.5 %all-reduce.5.cloned.1.call-start = ((), (), s32[]{:S(2)}) async-start(), calls=%async_computation.4 | async-start | bytes 1048576 | tf_op jit(solution)/shard_map/psum | solution.py:15
Sparse Core Ops, SparseCore 0:
  9.9 67.4 all-gather.8
  79.9 62.3 all-gather.10
  144.9 62.3 all-gather.12
  209.7 62.3 all-gather.14
  279.5 45.0 all-reduce.6
  327.1 75.7 all-reduce.4
